TPU v7x, 256 devices: a whole 4x4x8 slice. The times are simulated.
256 devices in a mesh: dp: 16 (over y, x), expert: 16 (over z, core).
Axes of the slice: x: 4, y: 4, z: 8, core: 2. Of those that a mesh axis runs over, the one named last changes fastest.
Arguments:
- tokens: bfloat16 [12288, 2048], P(('dp', 'expert')), may hold values from -6 to 6
- routes: int32 [12288, 8], P(('dp', 'expert')), may hold values from 0 to 15, all different within a row; in each aligned block of 48 rows (0 to 47, 48 to 95, ...) at most 32 rows name the same one
- route_weights: float32 [12288, 8], P(('dp', 'expert')), may hold values from 0.1 to 1
- cotangent: bfloat16 [12288, 2048], P(('dp', 'expert')), may hold values from -1.5 to 1.5
- gate_weight: bfloat16 [16, 2048, 768], P('expert', 'dp'), may hold values from -0.125 to 0.125
- up_weight: bfloat16 [16, 2048, 768], P('expert', 'dp'), may hold values from -0.125 to 0.125
- down_weight: bfloat16 [16, 768, 2048], P('expert', None, 'dp'), may hold values from -0.21875 to 0.21875
Outputs:
- mixed: bfloat16 [12288, 2048], P(('dp', 'expert'))
- input_grad: bfloat16 [12288, 2048], P(('dp', 'expert'))
- grad_gate: float32 [16, 2048, 768], P('expert', 'dp')
- grad_up: float32 [16, 2048, 768], P('expert', 'dp')
- grad_down: float32 [16, 768, 2048], P('expert', None, 'dp')
Inputs may be any that keep to these rules, and one draw needn't show every extreme that they name: `routes`: each row names 8 different experts. Among the 48 rows of one device no expert is named by more than 32 rows, and that bound is reached.
All inputs are finite; a program needn't handle non-finite values.
Results may differ from a plain program's by a relative error of at most 0.02.
Values may be sent and summed in bfloat16 or wider, within the bound.
No kernel may reach another device: no remote copies, remote signals or barrier semaphores. Data moves between devices by JAX's collectives and lax.ppermute only.
A program may use at most 128 MiB of HBM per device.

v0:
```python
import jax
import jax.numpy as jnp
from jax import lax
from jax.sharding import PartitionSpec as P


def dispatch_layout(routes, owners, capacity):
    token_count, slot_count = routes.shape
    pair_count = token_count * slot_count
    flat_routes = routes.reshape(pair_count)
    one_hot = (flat_routes[:, None] == jnp.arange(owners, dtype=jnp.int32)[None, :]).astype(
        jnp.int32
    )
    earlier = jnp.cumsum(one_hot, axis=0) - one_hot
    position = jnp.sum(earlier * one_hot, axis=1)
    destination = flat_routes * capacity + position
    slot_ids = jnp.arange(owners * capacity, dtype=jnp.int32)
    matches = destination[None, :] == slot_ids[:, None]
    filled = jnp.any(matches, axis=1)
    source = jnp.sum(
        jnp.where(matches, jnp.arange(pair_count, dtype=jnp.int32)[None, :], 0), axis=1
    )
    return (destination, filled, source)


def shards(tokens, routes, route_weights, cotangent, gate_weight, up_weight, down_weight):
    owners = lax.axis_size("expert")
    token_count, slot_count = routes.shape
    model_width = tokens.shape[1]
    hidden_units = gate_weight.shape[2]
    capacity = min(token_count, 4 * token_count * slot_count // (3 * owners))
    destination, filled, source = dispatch_layout(routes, owners, capacity)
    token_index = source // slot_count
    send_rows = jnp.where(filled[:, None], tokens[token_index], jnp.zeros((), tokens.dtype))
    send_rows = send_rows.reshape(owners, capacity, model_width)
    slot_weight = jnp.where(filled, route_weights.reshape(-1)[source], jnp.float32(0.0))
    send_scaled = (slot_weight[:, None] * cotangent[token_index].astype(jnp.float32)).astype(
        jnp.bfloat16
    )
    send_scaled = send_scaled.reshape(owners, capacity, model_width)
    contract_last = (((1,), (1,)), ((), ()))
    contract_first = (((0,), (0,)), ((), ()))
    whole_gate, whole_up, whole_down = (
        lax.all_gather(gate_weight, "dp", axis=1, tiled=True),
        lax.all_gather(up_weight, "dp", axis=1, tiled=True),
        lax.all_gather(down_weight, "dp", axis=2, tiled=True),
    )
    arrived = lax.all_to_all(send_rows, "expert", split_axis=0, concat_axis=0, tiled=True).reshape(
        -1, model_width
    )
    gate_proj = jnp.dot(arrived, whole_gate[0], preferred_element_type=jnp.float32)
    up_proj = jnp.dot(arrived, whole_up[0], preferred_element_type=jnp.float32)
    sigmoid_gate = jax.nn.sigmoid(gate_proj)
    activation = gate_proj * sigmoid_gate
    hidden = (activation * up_proj).astype(jnp.bfloat16)
    outputs = jnp.dot(hidden, whole_down[0], preferred_element_type=jnp.float32).astype(
        jnp.bfloat16
    )
    gate_proj, up_proj, sigmoid_gate, activation, hidden, outputs = (
        gate_proj,
        up_proj,
        sigmoid_gate,
        activation,
        hidden,
        outputs,
    )
    back_outputs = lax.all_to_all(
        outputs.reshape(owners, capacity, model_width),
        "expert",
        split_axis=0,
        concat_axis=0,
        tiled=True,
    )
    scaled = lax.all_to_all(send_scaled, "expert", split_axis=0, concat_axis=0, tiled=True).reshape(
        -1, model_width
    )
    hidden_grad = lax.dot_general(
        scaled, whole_down[0], contract_last, preferred_element_type=jnp.float32
    )
    derivative = sigmoid_gate * (1.0 + gate_proj * (1.0 - sigmoid_gate))
    gate_grad = (hidden_grad * up_proj * derivative).astype(jnp.bfloat16)
    up_grad = (hidden_grad * activation).astype(jnp.bfloat16)
    both_grads = jnp.concatenate([gate_grad, up_grad], axis=1)
    slot_grads = lax.dot_general(
        gate_grad, whole_gate[0], contract_last, preferred_element_type=jnp.float32
    )
    slot_grads = slot_grads + lax.dot_general(
        up_grad, whole_up[0], contract_last, preferred_element_type=jnp.float32
    )
    slot_grads = slot_grads.astype(jnp.bfloat16)
    summed = lax.psum_scatter(
        jnp.concatenate(
            [
                lax.dot_general(
                    arrived, both_grads, contract_first, preferred_element_type=jnp.float32
                ),
                lax.dot_general(scaled, hidden, contract_first, preferred_element_type=jnp.float32),
            ],
            axis=1,
        ).astype(jnp.bfloat16),
        "dp",
        scatter_dimension=0,
        tiled=True,
    ).astype(jnp.float32)
    slot_grads, summed = (slot_grads, summed)
    back_grads = lax.all_to_all(
        slot_grads.reshape(owners, capacity, model_width),
        "expert",
        split_axis=0,
        concat_axis=0,
        tiled=True,
    )
    returned = back_outputs.reshape(-1, model_width)[destination].reshape(
        token_count, slot_count, model_width
    )
    mixed = jnp.sum(route_weights[:, :, None] * returned.astype(jnp.float32), axis=1).astype(
        jnp.bfloat16
    )
    grads_home = back_grads.reshape(-1, model_width)[destination].reshape(
        token_count, slot_count, model_width
    )
    input_grad = jnp.sum(grads_home.astype(jnp.float32), axis=1).astype(jnp.bfloat16)
    grad_gate = summed[:, :hidden_units][None]
    grad_up = summed[:, hidden_units : 2 * hidden_units][None]
    grad_down = summed[:, 2 * hidden_units :].T[None]
    return (mixed, input_grad, grad_gate, grad_up, grad_down)


def solution(mesh):
    placed = (
        P(("dp", "expert"), None),
        P(("dp", "expert"), None),
        P(("dp", "expert"), None),
        P(("dp", "expert"), None),
        P("expert", "dp", None),
        P("expert", "dp", None),
        P("expert", None, "dp"),
    )
    return jax.shard_map(
        shards,
        mesh=mesh,
        in_specs=placed,
        out_specs=(
            P(("dp", "expert"), None),
            P(("dp", "expert"), None),
            P("expert", "dp", None),
            P("expert", "dp", None),
            P("expert", None, "dp"),
        ),
        check_vma=False,
    )
```

profile of v0, /device:TPU:1, one launch (start us, length us, event | category | flops | bytes accessed | tf_op | source)
XLA Modules:
  0.0 355.8 jit_solution(11340861245392224770)
XLA Ops:
  7.2 0.0 copy-start
  7.2 0.0 all-gather.8.cloned.1.call-start
  7.2 0.7 all-gather.8.cloned.1.call-update
  7.9 0.0 all-gather.6.cloned.1.call-start
  8.0 0.7 all-gather.6.cloned.1.call-update
  8.7 0.8 copy.32
  9.4 0.1 reshape.186
  9.5 0.1 eq.39
  9.6 0.8 copy.31
  10.4 0.1 reshape.191
  10.5 0.9 reduce-window.6
  11.4 0.2 slice_reduce_fusion
  11.6 0.1 fusion.26
  11.7 0.2 fusion.23
  11.9 0.1 broadcast_in_dim.51
  12.0 0.2 select_reduce_fusion
  12.2 3.5 gather_fusion.2
  15.7 0.1 gather.23
  15.8 0.0 copy-done
  15.8 2.5 gather_fusion.3
  18.2 1.7 fusion
  20.0 10.1 %all-to-all-start.2 = ((bf16[16,32,2048]{2,1,0:T(8,128)(2,1)}), bf16[16,32,2048]{2,1,0:T(8,128)(2,1)}, u32[]{:S(2)}, u32[]{:S(2)}) async-start(bf16[16,32,2048]{2,1,0:T(8,128)(2,1)} %fusion), calls=%async_computation.2 | async-start | bytes 4194304 | tf_op jit(solution)/shard_map/all_to_all | solution.py:74
  30.1 0.0 all-gather.4.cloned.1.call-start
  30.1 0.7 all-gather.4.cloned.1.call-update
  30.8 0.0 copy-done.2
  30.8 2.5 gather_fusion
  33.3 1.5 broadcast_select_fusion
  34.8 44.3 %all-to-all-done.2 = bf16[16,32,2048]{2,1,0:T(8,128)(2,1)} async-done(((bf16[16,32,2048]{2,1,0:T(8,128)(2,1)}), bf16[16,32,2048]{2,1,0:T(8,128)(2,1)}, u32[]{:S(2)}, u32[]{:S(2)}) %all-to-all-start.2) | async-done | bytes 2097184 | tf_op jit(solution)/shard_map/all_to_all | solution.py:74
  79.1 5.0 %all-to-all-start = ((bf16[16,32,2048]{2,1,0:T(8,128)(2,1)}), bf16[16,32,2048]{2,1,0:T(8,128)(2,1)S(1)}, u32[]{:S(2)}, u32[]{:S(2)}) async-start(bf16[16,32,2048]{2,1,0:T(8,128)(2,1)} %broadcast_select_fusion), calls=%async_computation | async-start | bytes 4194304 | tf_op jit(solution)/shard_map/all_to_all | solution.py:48
  84.1 0.0 reduce-scatter.4.cloned.1.call-start
  84.2 0.0 all-gather.8.cloned.1.call-done
  84.2 5.6 %fusion.2 = f32[512,768]{1,0:T(8,128)} fusion(bf16[512,2048]{1,0:T(8,128)(2,1)} %bitcast.13, bf16[1,768,2048]{2,1,0:T(8,128)(2,1)} %all-gather.8.cloned.1.call-done), kind=kOutput, calls=%fused_computation.13 | convolution fusion | flops 1610612736 | bytes 6815744 | tf_op jit(solution)/shard_map/dot_general | solution.py:77
  89.8 43.3 %all-to-all-done = bf16[16,32,2048]{2,1,0:T(8,128)(2,1)S(1)} async-done(((bf16[16,32,2048]{2,1,0:T(8,128)(2,1)}), bf16[16,32,2048]{2,1,0:T(8,128)(2,1)S(1)}, u32[]{:S(2)}, u32[]{:S(2)}) %all-to-all-start) | async-done | bytes 2097184 | tf_op jit(solution)/shard_map/all_to_all | solution.py:48
  133.1 4.8 %fusion.8 = f32[512,768]{1,0:T(8,128)} fusion(bf16[512,2048]{1,0:T(8,128)(2,1)S(1)} %bitcast.79, bf16[1,2048,768]{2,1,0:T(8,128)(2,1)} %all-gather.6.cloned.1.call-done), kind=kOutput, calls=%fused_computation.19 | convolution fusion | flops 1610612736 | bytes 6815744 | tf_op jit(solution)/shard_map/dot_general | solution.py:52
  137.9 42.9 %all-gather.4.cloned.1.call-done = bf16[1,2048,768]{2,1,0:T(8,128)(2,1)} async-done(((bf16[1,128,768]{2,1,0:T(8,128)(2,1)}), bf16[1,2048,768]{2,1,0:T(8,128)(2,1)}) %all-gather.4.cloned.1.call-update) | async-done | bytes 3145744 | tf_op jit(solution)/shard_map/all_gather | solution.py:44
  180.8 5.2 %multiply_convert_fusion.1 = (bf16[512,768]{1,0:T(8,128)(2,1)S(1)}, bf16[512,768]{1,0:T(8,128)(2,1)S(1)}, bf16[512,768]{1,0:T(8,128)(2,1)S(1)}) fusion(f32[512,768]{1,0:T(8,128)} %fusion.2, f32[512,768]{1,0:T(8,128)} %fusion.8, bf16[512,2048]{1,0:T(8,128)(2,1)S(1)} %bitcast.80, bf16[1,2048,768]{2,1,0:T(8,128)(2,1)} %all-gather.4.cloned.1.call-done), kind=kOutput, calls=%fused_computation.32 | convolution fusion | flops 1616510976 | bytes 10747904 | tf_op jit(solution)/shard_map/dot_general | solution.py:51
  186.0 0.0 copy-start.7
  186.0 0.0 copy-start.6
  186.0 4.0 %convolution_convert_fusion.1 = bf16[2048,768]{0,1:T(8,128)(2,1)S(1)} fusion(bf16[512,2048]{1,0:T(8,128)(2,1)} %bitcast.13, bf16[512,768]{1,0:T(8,128)(2,1)S(1)} %get-tuple-element.27), kind=kOutput, calls=%fused_computation.10 | convolution fusion | flops 1612185600 | bytes 6029312 | tf_op jit(solution)/shard_map/dot_general | solution.py:97
  190.1 3.9 %convolution_convert_fusion = bf16[2048,1536]{0,1:T(8,128)(2,1)S(1)} fusion(bf16[512,2048]{1,0:T(8,128)(2,1)S(1)} %bitcast.81, bf16[512,768]{1,0:T(8,128)(2,1)S(1)} %get-tuple-element.26, bf16[512,768]{1,0:T(8,128)(2,1)S(1)} %get-tuple-element.25), kind=kOutput, calls=%fused_computation.6 | convolution fusion | flops 3227516928 | bytes 9961472 | tf_op jit(solution)/shard_map/dot_general | solution.py:94
  194.0 11.3 %pad_maximum_fusion = bf16[2048,2304]{0,1:T(8,128)(2,1)} fusion(bf16[2048,768]{0,1:T(8,128)(2,1)S(1)} %convolution_convert_fusion.1, bf16[2048,1536]{0,1:T(8,128)(2,1)S(1)} %convolution_convert_fusion), kind=kLoop, calls=%fused_computation.5 | loop fusion | flops 18874368 | bytes 18874368 | tf_op jit(solution)/shard_map/concatenate | solution.py:92
  205.3 12.4 %copy.39 = bf16[2048,2304]{1,0:T(8,128)(2,1)} copy(bf16[2048,2304]{0,1:T(8,128)(2,1)} %pad_maximum_fusion) | data formatting | bytes 18874368
  217.7 0.0 reduce-scatter.4.cloned.1.call-update
  217.8 1.1 copy-done.8
  218.9 5.0 %fusion.14 = bf16[512,2048]{1,0:T(8,128)(2,1)} fusion(bf16[512,768]{1,0:T(8,128)(2,1)S(1)} %copy-done.8, bf16[1,768,2048]{2,1,0:T(8,128)(2,1)} %all-gather.8.cloned.1.call-done), kind=kOutput, calls=%fused_computation.25 | convolution fusion | flops 1611661312 | bytes 6029312 | tf_op jit(solution)/shard_map/dot_general | solution.py:56
  223.9 8.0 %all-to-all-start.1 = ((bf16[16,32,2048]{2,1,0:T(8,128)(2,1)}), bf16[16,32,2048]{2,1,0:T(8,128)(2,1)S(1)}, u32[]{:S(2)}, u32[]{:S(2)}) async-start(bf16[16,32,2048]{2,1,0:T(8,128)(2,1)} %bitcast.83), calls=%async_computation.1 | async-start | bytes 4194304 | tf_op jit(solution)/shard_map/all_to_all | solution.py:67
  231.9 4.1 %fusion.6 = f32[512,2048]{1,0:T(8,128)S(1)} fusion(bf16[512,768]{1,0:T(8,128)(2,1)} %copy-done.6, bf16[1,2048,768]{2,1,0:T(8,128)(2,1)} %all-gather.6.cloned.1.call-done), kind=kOutput, calls=%fused_computation.17 | convolution fusion | flops 1610612736 | bytes 8126464 | tf_op jit(solution)/shard_map/dot_general | solution.py:87
  236.0 3.3 add_convert_fusion
  239.3 41.5 %all-to-all-done.1 = bf16[16,32,2048]{2,1,0:T(8,128)(2,1)S(1)} async-done(((bf16[16,32,2048]{2,1,0:T(8,128)(2,1)}), bf16[16,32,2048]{2,1,0:T(8,128)(2,1)S(1)}, u32[]{:S(2)}, u32[]{:S(2)}) %all-to-all-start.1) | async-done | bytes 2097184 | tf_op jit(solution)/shard_map/all_to_all | solution.py:67
  280.8 5.1 %all-to-all-start.3 = ((bf16[16,32,2048]{2,1,0:T(8,128)(2,1)}), bf16[16,32,2048]{2,1,0:T(8,128)(2,1)}, u32[]{:S(2)}, u32[]{:S(2)}) async-start(bf16[16,32,2048]{2,1,0:T(8,128)(2,1)} %bitcast.82), calls=%async_computation.3 | async-start | bytes 4194304 | tf_op jit(solution)/shard_map/all_to_all | solution.py:106
  286.0 0.1 copy.35
  286.0 0.1 mul.73
  286.2 3.1 gather_fusion.1
  289.3 45.7 %all-to-all-done.3 = bf16[16,32,2048]{2,1,0:T(8,128)(2,1)} async-done(((bf16[16,32,2048]{2,1,0:T(8,128)(2,1)}), bf16[16,32,2048]{2,1,0:T(8,128)(2,1)}, u32[]{:S(2)}, u32[]{:S(2)}) %all-to-all-start.3) | async-done | bytes 2097184 | tf_op jit(solution)/shard_map/all_to_all | solution.py:106
  335.0 6.3 %gather_fusion.4 = bf16[384,2048]{1,0:T(8,128)(2,1)S(1)} fusion(bf16[512,2048]{1,0:T(8,128)(2,1)} %bitcast.15, s32[1024]{0:T(1024)S(1)} %pad_clamp_fusion.1), kind=kCustom, calls=%fused_computation.4 | custom fusion | bytes 3147264 | tf_op jit(solution)/shard_map/gather | solution.py:119
  341.3 1.7 bitcast_reduce_fusion
  343.0 2.1 fusion.1
  345.1 1.4 copy.40
  346.5 0.0 copy-start.1
  346.5 0.1 convert_element_type.61
  346.6 0.8 slice_bitcast_fusion
  347.4 0.9 copy.38
  348.3 0.9 copy.37
  349.2 0.0 copy-done.1
  (22 shorter events, 0.1 us)
Async XLA Ops:
  7.2 8.6 %copy-start = (bf16[48,2048]{1,0:T(8,128)(2,1)S(1)}, bf16[48,2048]{1,0:T(8,128)(2,1)}, u32[]{:S(2)}) copy-start(bf16[48,2048]{1,0:T(8,128)(2,1)} %param.10) | copy-start | bytes 589828
  7.2 77.0 %all-gather.8.cloned.1.call-start = ((), (), s32[]{:S(2)}) async-start(), calls=%async_computation.7 | async-start | bytes 3342336 | tf_op jit(solution)/shard_map/all_gather | solution.py:46
  7.9 125.2 %all-gather.6.cloned.1.call-start = ((), (), s32[]{:S(2)}) async-start(), calls=%async_computation.6 | async-start | bytes 3342336 | tf_op jit(solution)/shard_map/all_gather | solution.py:45
  20.0 10.9 %copy-start.2 = (bf16[48,2048]{1,0:T(8,128)(2,1)S(1)}, bf16[48,2048]{1,0:T(8,128)(2,1)}, u32[]{:S(2)}) copy-start(bf16[48,2048]{1,0:T(8,128)(2,1)} %param.7) | copy-start | bytes 589828
  20.0 59.2 %all-to-all-start.2 = ((bf16[16,32,2048]{2,1,0:T(8,128)(2,1)}), bf16[16,32,2048]{2,1,0:T(8,128)(2,1)}, u32[]{:S(2)}, u32[]{:S(2)}) async-start(bf16[16,32,2048]{2,1,0:T(8,128)(2,1)} %fusion), calls=%async_computation.2 | async-start | bytes 4194304 | tf_op jit(solution)/shard_map/all_to_all | solution.py:74
  30.1 150.7 %all-gather.4.cloned.1.call-start = ((), (), s32[]{:S(2)}) async-start(), calls=%async_computation.5 | async-start | bytes 3342336 | tf_op jit(solution)/shard_map/all_gather | solution.py:44
  79.1 53.9 %all-to-all-start = ((bf16[16,32,2048]{2,1,0:T(8,128)(2,1)}), bf16[16,32,2048]{2,1,0:T(8,128)(2,1)S(1)}, u32[]{:S(2)}, u32[]{:S(2)}) async-start(bf16[16,32,2048]{2,1,0:T(8,128)(2,1)} %broadcast_select_fusion), calls=%async_computation | async-start | bytes 4194304 | tf_op jit(solution)/shard_map/all_to_all | solution.py:48
  84.1 261.0 %reduce-scatter.4.cloned.1.call-start = ((), (), s32[]{:S(2)}) async-start(), calls=%async_computation.8 | async-start | bytes 10027008
  186.0 4.0 %copy-start.7 = (bf16[512,768]{1,0:T(8,128)(2,1)}, bf16[512,768]{1,0:T(8,128)(2,1)S(1)}, u32[]{:S(2)}) copy-start(bf16[512,768]{1,0:T(8,128)(2,1)S(1)} %get-tuple-element.27) | copy-start | bytes 2359300
  186.0 4.0 %copy-start.6 = (bf16[512,768]{1,0:T(8,128)(2,1)}, bf16[512,768]{1,0:T(8,128)(2,1)S(1)}, u32[]{:S(2)}) copy-start(bf16[512,768]{1,0:T(8,128)(2,1)S(1)} %get-tuple-element.26) | copy-start | bytes 2359300
  217.7 1.1 copy-start.8
  223.9 57.0 %all-to-all-start.1 = ((bf16[16,32,2048]{2,1,0:T(8,128)(2,1)}), bf16[16,32,2048]{2,1,0:T(8,128)(2,1)S(1)}, u32[]{:S(2)}, u32[]{:S(2)}) async-start(bf16[16,32,2048]{2,1,0:T(8,128)(2,1)} %bitcast.83), calls=%async_computation.1 | async-start | bytes 4194304 | tf_op jit(solution)/shard_map/all_to_all | solution.py:67
  231.9 4.1 %copy-start.5 = (bf16[1,2048,768]{2,1,0:T(8,128)(2,1)S(1)}, bf16[1,2048,768]{2,1,0:T(8,128)(2,1)}, u32[]{:S(2)}) copy-start(bf16[1,2048,768]{2,1,0:T(8,128)(2,1)} %all-gather.4.cloned.1.call-done) | copy-start | bytes 9437188
  280.8 5.1 %copy-start.4 = (s32[48,8]{0,1:T(8,128)S(1)}, s32[48,8]{0,1:T(8,128)}, u32[]{:S(2)}) copy-start(s32[48,8]{0,1:T(8,128)} %param.8) | copy-start | bytes 4612
  280.8 54.2 %all-to-all-start.3 = ((bf16[16,32,2048]{2,1,0:T(8,128)(2,1)}), bf16[16,32,2048]{2,1,0:T(8,128)(2,1)}, u32[]{:S(2)}, u32[]{:S(2)}) async-start(bf16[16,32,2048]{2,1,0:T(8,128)(2,1)} %bitcast.82), calls=%async_computation.3 | async-start | bytes 4194304 | tf_op jit(solution)/shard_map/all_to_all | solution.py:106
  341.3 1.8 copy-start.3
  346.5 2.8 copy-start.1
Sparse Core Ops, SparseCore 0:
  10.4 60.5 all-gather.7
  73.4 52.9 all-gather.5
  128.8 51.9 all-gather.3
  217.9 90.3 reduce-scatter.3
where the time goes:
time: 357 us; the launch traced here: 356 us
  waiting for transfers between devices  220 us (62%)
  local copies, waits for them, and re-layouts  37.7 us (11%)
  matrix products  36 us (10%)
  starting transfers between devices  28.4 us (8%)
  other arithmetic  19.9 us (6%)
  between operations  14 us (4%)
    all_to_all x1, waiting for transfers between devices, shards(): lax.all_to_all(slot_grads.reshape(owners, capacity, model_width), 'expert...  45.7 us
    all_to_all x1, waiting for transfers between devices, shards(): lax.all_to_all(send_scaled, 'expert', split_axis=0, concat_axis=0, tiled=...  44.3 us
    all_to_all x1, waiting for transfers between devices, shards(): lax.all_to_all(send_rows, 'expert', split_axis=0, concat_axis=0, tiled=True)  43.3 us
    all_gather x1, waiting for transfers between devices, shards(): lax.all_gather(gate_weight, 'dp', axis=1, tiled=True)  42.9 us
    all_to_all x1, waiting for transfers between devices, shards(): lax.all_to_all(outputs.reshape(owners, capacity, model_width), 'expert',...  41.5 us
    unnamed x24, local copies, waits for them, and re-layouts  18.3 us
    concatenate x1, other arithmetic, shards(): jnp.concatenate([lax.dot_general(arrived, both_grads, contract_first, pre...  11.3 us
    all_to_all x1, starting transfers between devices, shards(): lax.all_to_all(send_scaled, 'expert', split_axis=0, concat_axis=0, tiled=...  10.1 us
  transfers between devices with their start and end apart: 8, of which 5 were waited for; matrix products, arithmetic and copies ran while one was open for 14% of the time, Pallas kernels for 0%

commit v1 on v0

v1 whole, which is shorter than its diff:
```python
import functools

import jax
import jax.numpy as jnp
from jax import lax
from jax.experimental import pallas as pl
from jax.experimental.pallas import tpu as pltpu
from jax.sharding import PartitionSpec as P

SIDE = 4
BLOCKS = SIDE * SIDE
BF = jnp.bfloat16
F32 = jnp.float32
LANES = 128
NT = (((1,), (1,)), ((), ()))
MASKS = ((1, 3), (3, 1))


def params(mib=60):
    return pltpu.CompilerParams(vmem_limit_bytes=mib << 20)


def cost(flops, moved, special=0):
    return pl.CostEstimate(flops=flops, bytes_accessed=moved, transcendentals=special)


def shape_of(*shape, dtype=BF):
    return jax.ShapeDtypeStruct(shape, dtype)


SMEM = pl.BlockSpec(memory_space=pltpu.SMEM)
VMEM = pl.BlockSpec(memory_space=pltpu.VMEM)
ANY = pl.BlockSpec(memory_space=pl.ANY)


def exchange(value, axis, turn):
    experts = lax.axis_size("expert")
    pairs = []
    for spot in range(BLOCKS):
        y, x = divmod(spot, SIDE)
        for expert in range(experts):
            mask = MASKS[expert % 2][turn]
            other = (y ^ mask) * SIDE + x if axis == "y" else y * SIDE + (x ^ mask)
            pairs.append((spot * experts + expert, other * experts + expert))
    return lax.ppermute(value, ("dp", "expert"), pairs)


def swap_cores(value):
    experts = lax.axis_size("expert")
    return lax.ppermute(value, "expert", [(e, e ^ 1) for e in range(experts)])


def double(value, axis, turn):
    return value, exchange(value, axis, turn)


def join(pair):
    return jnp.concatenate(pair, axis=0)


def add_kernel(keep_a, keep_b, got_a, got_b, out_a, out_b):
    out_a[...] = (keep_a[...].astype(F32) + got_a[...].astype(F32)).astype(BF)
    out_b[...] = (keep_b[...].astype(F32) + got_b[...].astype(F32)).astype(BF)


def add_halves(keep, got):
    count, rows, columns = keep.shape
    half = count // 2
    near = pl.BlockSpec((1, rows, columns), lambda i: (i, 0, 0))
    far = pl.BlockSpec((1, rows, columns), lambda i: (i + half, 0, 0))
    return pl.pallas_call(
        add_kernel,
        out_shape=[shape_of(half, rows, columns)] * 2,
        grid=(half,),
        in_specs=[near, far, near, far],
        out_specs=[near, near],
        compiler_params=params(),
        cost_estimate=cost(count * rows * columns, 6 * count * rows * columns),
        name="add_halves",
    )(keep, keep, got, got)


def scatter(keep, send, axes):
    got = exchange(send, axes[0], 1)
    keep, send = add_halves(keep, got)
    got = exchange(send, axes[0], 0)
    keep, send = add_halves(keep, got)
    got = exchange(send, axes[1], 1)
    keep, send = add_halves(keep, got)
    return keep, exchange(send, axes[1], 0)


def weights_kernel(gate_ref, up_ref, down_ref, first_ref, second_ref):
    rows = gate_ref.shape[0]
    turned = down_ref[...].T
    first_ref[pl.ds(0, rows), :] = gate_ref[...]
    second_ref[pl.ds(0, rows), :] = up_ref[...]
    first_ref[pl.ds(rows, rows // 2), :] = turned[: rows // 2]
    second_ref[pl.ds(rows, rows // 2), :] = turned[rows // 2 :]


def tokens_kernel(token_ref, cot_ref, weight_ref, out_ref):
    width = token_ref.shape[1]
    out_ref[:, pl.ds(0, width)] = token_ref[...]
    out_ref[:, pl.ds(width, width)] = cot_ref[...]
    out_ref[:, pl.ds(2 * width, LANES)] = weight_ref[...]


def spread_weights(routes, route_weights, owners):
    expert = jnp.arange(owners, dtype=jnp.int32)
    chosen = jnp.sum(
        jnp.where(routes[:, :, None] == expert, route_weights[:, :, None], 0.0), axis=1
    )
    high = lax.reduce_precision(chosen, 8, 7)
    mid = lax.reduce_precision(chosen - high, 8, 7)
    last = chosen - high - mid
    packed = jnp.concatenate([high, mid, last], axis=1).astype(BF)
    return jnp.pad(packed, ((0, 0), (0, LANES - 3 * owners)))


def chosen_weight(who_ref, packed, owners):
    lane = lax.broadcasted_iota(jnp.int32, packed.shape, 1)
    mine = (lax.rem(lane, owners) == who_ref[0]) & (lane < 3 * owners)
    return jnp.sum(jnp.where(mine, packed.astype(F32), 0.0), axis=1, keepdims=True)


def turn_kernel(who_ref, token_ref, cot_ref, packed_ref, turned_ref, scaled_ref, scaled_turned_ref, *, owners):
    turned_ref[...] = token_ref[...].T
    weight = chosen_weight(who_ref, packed_ref[...], owners)
    scaled = (weight * cot_ref[...].astype(F32)).astype(BF)
    scaled_ref[...] = scaled
    scaled_turned_ref[...] = scaled.T


def collect(scratch, column, table_ref, line, near_ref, far_ref, size, first):
    half = BLOCKS // 2
    for i in range(BLOCKS):
        start = pl.multiple_of(table_ref[line, i] * LANES + first, size)
        value = near_ref[i] if i < half else far_ref[i - half]
        scratch[pl.ds(start, size), pl.ds(column, value.shape[1])] = value


def hand_out(scratch, table_ref, line, keep_ref, send_ref, size, first):
    half = BLOCKS // 2
    for i in range(BLOCKS):
        start = pl.multiple_of(table_ref[line, i] * LANES + first, size)
        value = scratch[pl.ds(start, size), :]
        if i < half:
            keep_ref[i] = value
        else:
            send_ref[i - half] = value


def forward_kernel(
    table_ref, token_ref, turned_ref, g0, g1, u0, u1,
    hidden_ref, act_ref, slope_ref, ka, sa, kb, sb, weight_s, part_s,
):
    tile = hidden_ref.shape[1]
    collect(weight_s, 0, table_ref, 0, g0, g1, LANES, 0)
    collect(weight_s, tile, table_ref, 1, u0, u1, LANES, 0)
    both = jnp.dot(token_ref[...], weight_s[...], preferred_element_type=F32)
    gate, up = both[:, :tile], both[:, tile:]
    sigmoid = 1.0 / (1.0 + jnp.exp(-gate))
    act = gate * sigmoid
    hidden_ref[...] = (act * up).astype(BF)
    act_ref[...] = act
    slope_ref[...] = up * sigmoid * (1.0 + gate * (1.0 - sigmoid))
    part_s[...] = jnp.dot(
        turned_ref[...], hidden_ref[...], preferred_element_type=F32
    ).astype(BF)
    hand_out(part_s, table_ref, 0, ka, sa, LANES // 2, 0)
    hand_out(part_s, table_ref, 1, kb, sb, LANES // 2, LANES // 2)


def backward_kernel(
    table_ref, scaled_ref, act_ref, slope_ref, da0, da1, db0, db1, gate_ref, up_ref, down_s
):
    collect(down_s, 0, table_ref, 0, da0, da1, LANES // 2, 0)
    collect(down_s, 0, table_ref, 1, db0, db1, LANES // 2, LANES // 2)
    grad = jnp.dot(scaled_ref[...], down_s[...], preferred_element_type=F32)
    gate_ref[...] = (grad * slope_ref[...]).astype(BF)
    up_ref[...] = (grad * act_ref[...]).astype(BF)


def weight_grad_kernel(table_ref, turned_ref, gate_ref, up_ref, kg, sg, ku, su, part_s):
    for line, grad_ref, keep_ref, send_ref in ((0, gate_ref, kg, sg), (1, up_ref, ku, su)):
        part_s[...] = jnp.dot(
            turned_ref[...], grad_ref[...], preferred_element_type=F32
        ).astype(BF)
        hand_out(part_s, table_ref, line, keep_ref, send_ref, LANES, 0)


def returns_kernel(
    who_ref, table_ref, hidden_ref, packed_ref, gate_ref, up_ref, g0, g1, u0, u1, da0, da1, db0, db1,
    keep_ref, send_ref, down_s, both_s, weight_s, value_s, sems, *, owners, home_rows, tile,
):
    half = BLOCKS // 2
    columns = hidden_ref.shape[1]

    def copies(near, far, line, size, first, column, target, sem):
        out = []
        for i in range(BLOCKS):
            start = pl.multiple_of(table_ref[line, i] * LANES + first, size)
            source = near.at[i] if i < half else far.at[i - half]
            out.append(
                pltpu.make_async_copy(
                    source, target.at[pl.ds(start, size), pl.ds(column, columns)], sem.at[i]
                )
            )
        return out

    down = copies(da0, da1, 0, LANES // 2, 0, 0, down_s, sems.at[0])
    down += copies(db0, db1, 1, LANES // 2, LANES // 2, 0, down_s, sems.at[1])
    weights = copies(g0, g1, 0, LANES, 0, 0, weight_s, sems.at[2])
    weights += copies(u0, u1, 1, LANES, 0, columns, weight_s, sems.at[3])
    for copy in down + weights:
        copy.start()
    both_s[:, pl.ds(0, columns)] = gate_ref[...]
    both_s[:, pl.ds(columns, columns)] = up_ref[...]
    core = lax.rem(who_ref[0], 2)
    width = down_s.shape[0]

    def store(value, column):
        value_s[...] = value.astype(BF)
        for z in range(owners // 2):
            rows = pl.ds(z * home_rows, home_rows)
            mine = pl.multiple_of((2 * z + core) * home_rows, 16)
            theirs = pl.multiple_of((2 * z + 1 - core) * home_rows, 16)
            keep_ref[rows, pl.ds(column, tile)] = value_s[pl.ds(mine, home_rows), :]
            send_ref[rows, pl.ds(column, tile)] = value_s[pl.ds(theirs, home_rows), :]

    weight = chosen_weight(who_ref, packed_ref[...], owners)
    for copy in down:
        copy.wait()
    for n in range(0, width, tile):
        value = lax.dot_general(
            hidden_ref[...], down_s[pl.ds(n, tile), :], NT, preferred_element_type=F32
        )
        store(weight * value, n)
    for copy in weights:
        copy.wait()
    for n in range(0, width, tile):
        value = lax.dot_general(
            both_s[...], weight_s[pl.ds(n, tile), :], NT, preferred_element_type=F32
        )
        store(value, width + n)


def last_kernel(gate_a, gate_b, up_a, up_b, gate_ref, up_ref):
    gate_ref[...] = gate_a[0].astype(F32) + gate_b[0].astype(F32)
    up_ref[...] = up_a[0].astype(F32) + up_b[0].astype(F32)


def last_down_kernel(first_a, first_b, second_a, second_b, out_ref):
    first = first_a[0].astype(F32) + first_b[0].astype(F32)
    second = second_a[0].astype(F32) + second_b[0].astype(F32)
    out_ref[...] = jnp.concatenate([first, second], axis=0).T


def block_table(spot, core):
    y, x = spot // SIDE, spot % SIDE
    marks = jnp.where(core == 0, jnp.array([0, 1, 3, 2]), jnp.array([0, 3, 1, 2]))
    slow, fast = jnp.repeat(marks, SIDE), jnp.tile(marks, SIDE)
    first = (y ^ slow) * SIDE + (x ^ fast)
    second = (y ^ fast) * SIDE + (x ^ slow)
    return jnp.stack([first, second]).astype(jnp.int32)


def shards(tokens, routes, route_weights, cotangent, gate_weight, up_weight, down_weight):
    owners = lax.axis_size("expert")
    home_rows, width = tokens.shape
    _, features, hidden_units = gate_weight.shape
    tile = 2 * LANES
    tiles = hidden_units // tile
    rows = home_rows * owners
    me = lax.axis_index("expert").astype(jnp.int32)
    who = me.reshape(1)
    table = block_table(lax.axis_index("dp"), me % 2)

    block = features + features // 2
    first, second = pl.pallas_call(
        weights_kernel,
        out_shape=[shape_of(block, hidden_units)] * 2,
        compiler_params=params(),
        cost_estimate=cost(0, 12 * features * hidden_units),
        name="pack_weights",
    )(gate_weight[0], up_weight[0], down_weight[0])

    packed = pl.pallas_call(
        tokens_kernel,
        out_shape=shape_of(home_rows, 2 * width + LANES),
        compiler_params=params(),
        cost_estimate=cost(0, 8 * home_rows * width),
        name="pack_tokens",
    )(tokens, cotangent, spread_weights(routes, route_weights, owners))
    everyone = lax.all_gather(packed, "expert", axis=0, tiled=True)

    def gather(value, axes):
        value = join(double(value[None], axes[0], 0))
        value = join(double(value, axes[0], 1))
        wide = join(double(value[:, :features], axes[1], 0))
        near, far = double(wide, axes[1], 1)
        narrow = join(double(value[:, features:], axes[1], 0))
        return (near, far) + double(narrow, axes[1], 1)

    g0, g1, da0, da1 = gather(first, "xy")
    u0, u1, db0, db1 = gather(second, "yx")

    packed_at = 2 * width // LANES
    column = pl.BlockSpec((rows, tile), lambda j: (0, j))
    line = pl.BlockSpec((tile, rows), lambda j: (j, 0))
    token_turned, scaled, scaled_turned = pl.pallas_call(
        functools.partial(turn_kernel, owners=owners),
        out_shape=[shape_of(width, rows), shape_of(rows, width), shape_of(width, rows)],
        grid=(width // tile,),
        in_specs=[
            SMEM,
            column,
            pl.BlockSpec((rows, tile), lambda j: (0, width // tile + j)),
            pl.BlockSpec((rows, LANES), lambda j: (0, packed_at)),
        ],
        out_specs=[line, column, line],
        compiler_params=params(),
        cost_estimate=cost(rows * width, 10 * rows * width),
        name="turn_and_scale",
    )(who, everyone, everyone, everyone)

    product = 2 * rows * width * hidden_units
    half = BLOCKS // 2

    def whole(*shape):
        return pl.BlockSpec(shape, lambda j: (0,) * len(shape))

    def blocks_of(size):
        return pl.BlockSpec((half, size, tile), lambda j: (0, 0, j))

    def blocks_shape(size):
        return shape_of(half, size, hidden_units)

    small = features // 2
    hidden, act, slope, ka, sa, kb, sb = pl.pallas_call(
        forward_kernel,
        out_shape=[shape_of(rows, hidden_units)]
        + [shape_of(rows, hidden_units, dtype=F32)] * 2
        + [blocks_shape(small)] * 4,
        grid=(tiles,),
        in_specs=[SMEM, whole(rows, width), whole(width, rows)] + [blocks_of(features)] * 4,
        out_specs=[column] * 3 + [blocks_of(small)] * 4,
        scratch_shapes=[pltpu.VMEM((width, 2 * tile), BF), pltpu.VMEM((width, tile), BF)],
        compiler_params=params(),
        cost_estimate=cost(3 * product, 4 * rows * width + 6 * width * hidden_units),
        name="forward_hidden",
    )(table, everyone, scaled_turned, g0, g1, u0, u1)

    gate_grad, up_grad = pl.pallas_call(
        backward_kernel,
        out_shape=[shape_of(rows, hidden_units)] * 2,
        grid=(tiles,),
        in_specs=[SMEM, whole(rows, width), column, column] + [blocks_of(small)] * 4,
        out_specs=[column] * 2,
        scratch_shapes=[pltpu.VMEM((width, tile), BF)],
        compiler_params=params(),
        cost_estimate=cost(product, 2 * rows * width + 2 * width * hidden_units),
        name="backward_hidden",
    )(table, scaled, act, slope, da0, da1, db0, db1)

    wide = 2 * tile
    keep, send = pl.pallas_call(
        functools.partial(returns_kernel, owners=owners, home_rows=home_rows, tile=wide),
        out_shape=[shape_of(rows // 2, 2 * width)] * 2,
        grid=(1,),
        in_specs=[
            SMEM,
            SMEM,
            whole(rows, hidden_units),
            pl.BlockSpec((rows, LANES), lambda j: (0, packed_at)),
            whole(rows, hidden_units),
            whole(rows, hidden_units),
        ]
        + [ANY] * 8,
        out_specs=[whole(rows // 2, 2 * width)] * 2,
        scratch_shapes=[
            pltpu.VMEM((width, hidden_units), BF),
            pltpu.VMEM((rows, 2 * hidden_units), BF),
            pltpu.VMEM((width, 2 * hidden_units), BF),
            pltpu.VMEM((rows, wide), BF),
            pltpu.SemaphoreType.DMA((4, BLOCKS)),
        ],
        compiler_params=params(),
        cost_estimate=cost(3 * product, 4 * rows * width + 6 * width * hidden_units),
        name="outputs_and_slots",
    )(who, table, hidden, everyone, gate_grad, up_grad, g0, g1, u0, u1, da0, da1, db0, db1)

    kg, sg, ku, su = pl.pallas_call(
        weight_grad_kernel,
        out_shape=[blocks_shape(features)] * 4,
        grid=(tiles,),
        in_specs=[SMEM, whole(width, rows), column, column],
        out_specs=[blocks_of(features)] * 4,
        scratch_shapes=[pltpu.VMEM((width, tile), BF)],
        compiler_params=params(),
        cost_estimate=cost(2 * product, 2 * rows * width + 4 * width * hidden_units),
        name="grad_gate_up_part",
    )(table, token_turned, gate_grad, up_grad)

    down_a, down_b = scatter(ka, sa, "yx"), scatter(kb, sb, "xy")
    gate_sum, up_sum = scatter(kg, sg, "yx"), scatter(ku, su, "xy")
    grad_down = pl.pallas_call(
        last_down_kernel,
        out_shape=shape_of(hidden_units, features, dtype=F32),
        compiler_params=params(),
        cost_estimate=cost(0, 10 * features * hidden_units),
        name="last_down",
    )(*down_a, *down_b)
    grad_gate, grad_up = pl.pallas_call(
        last_kernel,
        out_shape=[shape_of(features, hidden_units, dtype=F32)] * 2,
        compiler_params=params(),
        cost_estimate=cost(0, 20 * features * hidden_units),
        name="last_gate_up",
    )(*gate_sum, *up_sum)

    home = (keep.astype(F32) + swap_cores(send).astype(F32)).astype(BF)
    groups = [[e for e in range(owners) if e % 2 == core] for core in range(2)]
    home = lax.psum_scatter(
        home, "expert", scatter_dimension=0, axis_index_groups=groups, tiled=True
    )
    return (
        home[:, :width],
        home[:, width:],
        grad_gate[None],
        grad_up[None],
        grad_down[None],
    )


def solution(mesh):
    placed = (
        P(("dp", "expert"), None),
        P(("dp", "expert"), None),
        P(("dp", "expert"), None),
        P(("dp", "expert"), None),
        P("expert", "dp", None),
        P("expert", "dp", None),
        P("expert", None, "dp"),
    )
    return jax.shard_map(
        shards,
        mesh=mesh,
        in_specs=placed,
        out_specs=(
            P(("dp", "expert"), None),
            P(("dp", "expert"), None),
            P("expert", "dp", None),
            P("expert", "dp", None),
            P("expert", None, "dp"),
        ),
        check_vma=False,
    )
```

time: 357 us -> 235 us (0.66)
  waiting for transfers between devices: 220 us -> 51.9 us
  Pallas kernels: 0 us -> 95.7 us
  matrix products: 36 us -> 0 us
  local copies, waits for them, and re-layouts: 37.7 us -> 13.9 us
  starting transfers between devices: 28.4 us -> 42.9 us
  other arithmetic: 19.9 us -> 12 us
    all_to_all x4 -> x0, waiting for transfers between devices: 175 us -> none  [the longest x1 45.7 us: shards(): lax.all_to_all(slot_grads.reshape(owners, capacity, model_width), 'expert...]
    pallas_call x0 -> x21, Pallas kernels: none -> 95.7 us  [the longest x12 31.1 us: add_halves(): pl.pallas_call(add_kernel, out_shape=[shape_of(half, rows, columns)] * 2,...]
    ppermute x0 -> x29, waiting for transfers between devices: none -> 51.9 us  [the longest x28 46.4 us: exchange(): return lax.ppermute(value, ('dp', 'expert'), pairs)]
    all_gather x3 -> x1, waiting for transfers between devices: 42.9 us -> 0.01 us  [shards(): everyone = lax.all_gather(packed, 'expert', axis=0, tiled=True)]
    ppermute x0 -> x29, starting transfers between devices: none -> 42.9 us  [the longest x28 34.5 us: exchange(): return lax.ppermute(value, ('dp', 'expert'), pairs)]
    dot_general x8 -> x0, matrix products: 36 us -> none  [the longest x1 5.61 us: shards(): lax.dot_general(scaled, whole_down[0], contract_last, preferred_element_t...]
    all_to_all x4 -> x0, starting transfers between devices: 28.2 us -> none  [the longest x1 10.1 us: shards(): lax.all_to_all(send_scaled, 'expert', split_axis=0, concat_axis=0, tiled=...]
    gather x6 -> x0, local copies, waits for them, and re-layouts: 17.9 us -> none  [the longest x1 6.25 us: shards(): back_grads.reshape(-1, model_width)[destination]]
  transfers between devices with their start and end apart: 8 -> 31, of which waited for: 5 -> 9; matrix products, arithmetic and copies ran while one was open for 14% -> 3% of each run, Pallas kernels for 0% -> 30%
where the time goes in v1:
time: 235 us; the launch traced here: 231 us
  Pallas kernels  95.7 us (41%)
  waiting for transfers between devices  51.9 us (22%)
  starting transfers between devices  42.9 us (18%)
  between operations  14.3 us (6%)
  local copies, waits for them, and re-layouts  13.9 us (6%)
  other arithmetic  12 us (5%)
    ppermute x28, waiting for transfers between devices, exchange(): return lax.ppermute(value, ('dp', 'expert'), pairs)  46.4 us
    ppermute x28, starting transfers between devices, exchange(): return lax.ppermute(value, ('dp', 'expert'), pairs)  34.5 us
    pallas_call x12, Pallas kernels, add_halves(): pl.pallas_call(add_kernel, out_shape=[shape_of(half, rows, columns)] * 2,...  31.1 us
    pallas_call x1, Pallas kernels, shards(): pl.pallas_call(functools.partial(returns_kernel, owners=owners, home_rows...  15.9 us
    pallas_call x1, Pallas kernels, shards(): pl.pallas_call(forward_kernel, out_shape=[shape_of(rows, hidden_units)] +...  13.9 us
    unnamed x44, local copies, waits for them, and re-layouts  11.7 us
    pallas_call x1, Pallas kernels, shards(): pl.pallas_call(weight_grad_kernel, out_shape=[blocks_shape(features)] * 4...  9.58 us
    pallas_call x1, Pallas kernels, shards(): pl.pallas_call(functools.partial(turn_kernel, owners=owners), out_shape=[...  9.29 us
  transfers between devices with their start and end apart: 31, of which 9 were waited for; matrix products, arithmetic and copies ran while one was open for 3% of the time, Pallas kernels for 30%

profile of v1, /device:TPU:1, one launch (start us, length us, event | category | flops | bytes accessed | tf_op | source)
XLA Modules:
  0.0 230.7 jit_solution(16148989250207248035)
XLA Ops:
  8.8 1.8 pack_tokens.1
  10.7 2.0 pack_weights.1
  12.7 3.3 %collective-permute-start = (bf16[1,192,768]{2,1,0:T(8,128)(2,1)}, bf16[1,192,768]{2,1,0:T(8,128)(2,1)S(1)}, u32[]{:S(2)}, u32[]{:S(2)}) collective-permute-start(bf16[1,192,768]{2,1,0:T(8,128)(2,1)} %bitcast.9), channel_id=1, source_target_pairs={{0,16},{1,49},{2,18},{3,51},{4,20},{5,53},{6,22},{7,55},{8,24},{9,... | collective-permute-start | bytes 884744 | tf_op jit(solution)/shard_map/ppermute | solution.py:45
  16.0 2.7 %collective-permute-start.4 = (bf16[1,192,768]{2,1,0:T(8,128)(2,1)}, bf16[1,192,768]{2,1,0:T(8,128)(2,1)S(1)}, u32[]{:S(2)}, u32[]{:S(2)}) collective-permute-start(bf16[1,192,768]{2,1,0:T(8,128)(2,1)} %bitcast.13), channel_id=1, source_target_pairs={{0,64},{1,193},{2,66},{3,195},{4,68},{5,197},{6,70},{7,199},{8,72}... | collective-permute-start | bytes 884744 | tf_op jit(solution)/shard_map/ppermute | solution.py:45
  18.8 1.7 collective-permute-done
  20.4 1.0 pad_maximum_fusion.6
  21.9 1.1 collective-permute-done.4
  23.1 1.0 pad_maximum_fusion.7
  24.5 6.1 %collective-permute-done.1 = bf16[2,192,768]{2,1,0:T(8,128)(2,1)S(1)} collective-permute-done((bf16[2,192,768]{2,1,0:T(8,128)(2,1)S(1)}, bf16[2,192,768]{2,1,0:T(8,128)(2,1)S(1)}, u32[]{:S(2)}, u32[]{:S(2)}) %collective-permute-start.1) | collective-permute-done | bytes 589856 | tf_op jit(solution)/shard_map/ppermute | solution.py:45
  30.8 2.9 %collective-permute-start.2 = (bf16[4,128,768]{2,1,0:T(8,128)(2,1)S(1)}, bf16[4,128,768]{2,1,0:T(8,128)(2,1)S(1)}, u32[]{:S(2)}, u32[]{:S(2)}) collective-permute-start(bf16[4,128,768]{2,1,0:T(8,128)(2,1)S(1)} %slice.24), channel_id=1, source_target_pairs={{0,64},{1,193},{2,66},{3,195},{4,68},{5,197},{6,70},{7,199},{8,72}... | collective-permute-start | bytes 2359304 | tf_op jit(solution)/shard_map/ppermute | solution.py:45
  34.0 2.6 %collective-permute-start.6 = (bf16[4,128,768]{2,1,0:T(8,128)(2,1)S(1)}, bf16[4,128,768]{2,1,0:T(8,128)(2,1)S(1)}, u32[]{:S(2)}, u32[]{:S(2)}) collective-permute-start(bf16[4,128,768]{2,1,0:T(8,128)(2,1)S(1)} %slice.25), channel_id=1, source_target_pairs={{0,16},{1,49},{2,18},{3,51},{4,20},{5,53},{6,22},{7,55},{8,24},{9,... | collective-permute-start | bytes 2359304 | tf_op jit(solution)/shard_map/ppermute | solution.py:45
  36.5 8.8 %collective-permute-done.2 = bf16[4,128,768]{2,1,0:T(8,128)(2,1)S(1)} collective-permute-done((bf16[4,128,768]{2,1,0:T(8,128)(2,1)S(1)}, bf16[4,128,768]{2,1,0:T(8,128)(2,1)S(1)}, u32[]{:S(2)}, u32[]{:S(2)}) %collective-permute-start.2) | collective-permute-done | bytes 786464 | tf_op jit(solution)/shard_map/ppermute | solution.py:45
  45.4 1.3 pad_maximum_fusion.g0
  46.8 1.4 pad_maximum_fusion.1.u0
  48.2 2.3 collective-permute-start.10
  50.5 1.3 collective-permute-start.8
  52.1 4.4 %collective-permute-done.10 = bf16[4,64,768]{2,1,0:T(8,128)(2,1)S(1)} collective-permute-done((bf16[4,64,768]{2,1,0:T(8,128)(2,1)S(1)}, bf16[4,64,768]{2,1,0:T(8,128)(2,1)S(1)}, u32[]{:S(2)}, u32[]{:S(2)}) %collective-permute-start.10) | collective-permute-done | bytes 393248 | tf_op jit(solution)/shard_map/ppermute | solution.py:45
  56.6 1.5 collective-permute-start.11
  58.1 5.0 %collective-permute-done.8 = bf16[4,64,768]{2,1,0:T(8,128)(2,1)S(1)} collective-permute-done((bf16[4,64,768]{2,1,0:T(8,128)(2,1)S(1)}, bf16[4,64,768]{2,1,0:T(8,128)(2,1)S(1)}, u32[]{:S(2)}, u32[]{:S(2)}) %collective-permute-start.8) | collective-permute-done | bytes 393248 | tf_op jit(solution)/shard_map/ppermute | solution.py:45
  64.0 9.3 %turn_and_scale.1 = (bf16[2048,768]{1,0:T(8,128)(2,1)}, bf16[768,2048]{1,0:T(8,128)(2,1)}, bf16[2048,768]{1,0:T(8,128)(2,1)}) custom-call(s32[1]{0:T(128)} %bitcast.who_ref, bf16[768,4224]{1,0:T(8,128)(2,1)} %all-gather.2.cloned.1.call-done.token_ref.cot_ref.packed_ref, bf16[768,4224]{1,0:T(8,128)(2,1)} %all-gather.2.cloned.1.call-done.token_ref.cot_ref.packed_ref, ...), custom_call_target="tpu_custom_call" | custom-call | flops 1572864 | bytes 15728640 | tf_op jit(solution)/shard_map/turn_and_scale/pallas_call | solution.py:312
  73.3 13.9 %forward_hidden.1 = (bf16[768,768]{1,0:T(8,128)(2,1)}, f32[768,768]{1,0:T(8,128)}, f32[768,768]{1,0:T(8,128)}, bf16[8,64,768]{2,1,0:T(8,128)(2,1)}, bf16[8,64,76...) custom-call(s32[2,16]{1,0:T(2,128)} %pad_add_fusion.table_ref, ...), custom_call_target="tpu_custom_call" | custom-call | flops 7247757312 | bytes 15728640 | tf_op jit(solution)/shard_map/forward_hidden/pallas_call | solution.py:341
  87.3 0.9 copy-done.13
  88.2 8.1 %backward_hidden.1 = (bf16[768,768]{1,0:T(8,128)(2,1)}, bf16[768,768]{1,0:T(8,128)(2,1)}) custom-call(s32[2,16]{1,0:T(2,128)} %pad_add_fusion.table_ref, bf16[768,2048]{1,0:T(8,128)(2,1)} %get-tuple-element.55.scaled_ref, f32[768,768]{1,0:T(8,128)} %get-tuple-element.56.act_ref, f32[768,768]{1,0:T(8,128)} %get-tuple-element.57.slope_ref, ...), custom_call_target="tpu_custom_call" | custom-call | flops 2415919104 | bytes 6291456 | tf_op jit(solution)/shard_map/backward_hidden/pallas_call | solution.py:355
  96.3 15.9 %outputs_and_slots.1 = (bf16[384,4096]{1,0:T(8,128)(2,1)}, bf16[384,4096]{1,0:T(8,128)(2,1)}) custom-call(s32[1]{0:T(128)} %bitcast.who_ref, s32[2,16]{1,0:T(2,128)} %pad_add_fusion.table_ref, bf16[768,768]{1,0:T(8,128)(2,1)} %get-tuple-element.54.hidden_ref, bf16[768,4224]{1,0:T(8,128)(2,1)} %all-gather.2.cloned.1.call-done.token_ref.cot_ref.packed_ref, ...), custom_call_target="tpu_custom_call" | custom-call | flops 7247757312 | bytes 15728640 | tf_op jit(solution)/shard_map/outputs_and_slots/pallas_call | solution.py:368
  112.2 8.3 %collective-permute-start.12 = (bf16[384,4096]{1,0:T(8,128)(2,1)}, bf16[384,4096]{1,0:T(8,128)(2,1)S(1)}, u32[]{:S(2)}, u32[]{:S(2)}) collective-permute-start(bf16[384,4096]{1,0:T(8,128)(2,1)} %get-tuple-element.61), channel_id=1, source_target_pairs={{0,1},{1,0},{2,3},{3,2},{4,5},{5,4},{6,7},{7,6},{8,9},{9,8},{10,11... | collective-permute-start | bytes 9437192 | tf_op jit(solution)/shard_map/ppermute | solution.py:50
  120.5 5.5 %collective-permute-done.12 = bf16[384,4096]{1,0:T(8,128)(2,1)S(1)} collective-permute-done((bf16[384,4096]{1,0:T(8,128)(2,1)}, bf16[384,4096]{1,0:T(8,128)(2,1)S(1)}, u32[]{:S(2)}, u32[]{:S(2)}) %collective-permute-start.12) | collective-permute-done | bytes 3145760 | tf_op jit(solution)/shard_map/ppermute | solution.py:50
  126.0 4.7 %add_convert_fusion = bf16[384,4096]{1,0:T(8,128)(2,1)} fusion(bf16[384,4096]{1,0:T(8,128)(2,1)S(1)} %collective-permute-done.12, bf16[384,4096]{1,0:T(8,128)(2,1)} %get-tuple-element.60), kind=kLoop, calls=%fused_computation | loop fusion | flops 6291456 | bytes 9437184 | tf_op jit(solution)/shard_map/convert_element_type | solution.py:423
  130.8 9.6 %grad_gate_up_part.1 = (bf16[8,128,768]{2,1,0:T(8,128)(2,1)}, bf16[8,128,768]{2,1,0:T(8,128)(2,1)}, bf16[8,128,768]{2,1,0:T(8,128)(2,1)}, bf16[8,128,768]{2,1,0:T(8,128)(2,1)}) custom-call(s32[2,16]{1,0:T(2,128)} %pad_add_fusion.table_ref, bf16[2048,768]{1,0:T(8,128)(2,1)} %get-tuple-element.62.turned_ref, bf16[768,768]{1,0:T(8,128)(2,1)} %get-tuple-element.58.gate_ref, ...), custom_call_target="tpu_custom_call" | custom-call | flops 4831838208 | bytes 9437184 | tf_op jit(solution)/shard_map/grad_gate_up_part/pallas_call | solution.py:394
  140.5 1.4 collective-permute-start.25
  141.8 1.5 collective-permute-start.21
  143.3 16.9 %collective-permute-done.17.got_a.got_b = bf16[8,128,768]{2,1,0:T(8,128)(2,1)S(1)} collective-permute-done((bf16[8,128,768]{2,1,0:T(8,128)(2,1)}, bf16[8,128,768]{2,1,0:T(8,128)(2,1)S(1)}, u32[]{:S(2)}, u32[]{:S(2)}) %collective-permute-start.17) | collective-permute-done | bytes 1572896 | tf_op jit(solution)/shard_map/ppermute | solution.py:45
  160.2 1.3 copy-done.1
  161.5 4.0 %add_halves.15 = (bf16[4,128,768]{2,1,0:T(8,128)(2,1)}, bf16[4,128,768]{2,1,0:T(8,128)(2,1)}) custom-call(bf16[8,128,768]{2,1,0:T(8,128)(2,1)} %get-tuple-element.71.keep_a.keep_b, bf16[8,128,768]{2,1,0:T(8,128)(2,1)} %get-tuple-element.71.keep_a.keep_b, bf16[8,128,768]{2,1,0:T(8,128)(2,1)} %copy-done.1, bf16[8,128,768]{2,1,0:T(8,128)(2,1)} %copy-done.1), custom_call_target="tpu_custom_call" | custom-call | flops 786432 | bytes 4718592 | tf_op jit(solution)/shard_map/add_halves/pallas_call | solution.py:71
  165.5 1.2 copy-done
  166.7 4.0 %add_halves.12 = (bf16[4,128,768]{2,1,0:T(8,128)(2,1)}, bf16[4,128,768]{2,1,0:T(8,128)(2,1)}) custom-call(bf16[8,128,768]{2,1,0:T(8,128)(2,1)} %get-tuple-element.63.keep_a.keep_b, bf16[8,128,768]{2,1,0:T(8,128)(2,1)} %get-tuple-element.63.keep_a.keep_b, bf16[8,128,768]{2,1,0:T(8,128)(2,1)} %copy-done, bf16[8,128,768]{2,1,0:T(8,128)(2,1)} %copy-done), custom_call_target="tpu_custom_call" | custom-call | flops 786432 | bytes 4718592 | tf_op jit(solution)/shard_map/add_halves/pallas_call | solution.py:71
  170.7 1.3 collective-permute-start.14
  172.0 3.6 %add_halves.21 = (bf16[4,64,768]{2,1,0:T(8,128)(2,1)}, bf16[4,64,768]{2,1,0:T(8,128)(2,1)}) custom-call(bf16[8,64,768]{2,1,0:T(8,128)(2,1)} %get-tuple-element.89.keep_a.keep_b, bf16[8,64,768]{2,1,0:T(8,128)(2,1)} %get-tuple-element.89.keep_a.keep_b, bf16[8,64,768]{2,1,0:T(8,128)(2,1)} %collective-permute-done.25.got_a.got_b, ...), custom_call_target="tpu_custom_call" | custom-call | flops 393216 | bytes 2359296 | tf_op jit(solution)/shard_map/add_halves/pallas_call | solution.py:71
  175.6 1.4 collective-permute-start.26
  177.0 0.9 copy-done.6
  177.9 3.5 %add_halves.18 = (bf16[4,64,768]{2,1,0:T(8,128)(2,1)}, bf16[4,64,768]{2,1,0:T(8,128)(2,1)}) custom-call(bf16[8,64,768]{2,1,0:T(8,128)(2,1)} %get-tuple-element.81.keep_a.keep_b, bf16[8,64,768]{2,1,0:T(8,128)(2,1)} %get-tuple-element.81.keep_a.keep_b, bf16[8,64,768]{2,1,0:T(8,128)(2,1)} %copy-done.6, bf16[8,64,768]{2,1,0:T(8,128)(2,1)} %copy-done.6), custom_call_target="tpu_custom_call" | custom-call | flops 393216 | bytes 2359296 | tf_op jit(solution)/shard_map/add_halves/pallas_call | solution.py:71
  181.4 2.7 %collective-permute-start.22 = (bf16[4,64,768]{2,1,0:T(8,128)(2,1)}, bf16[4,64,768]{2,1,0:T(8,128)(2,1)S(1)}, u32[]{:S(2)}, u32[]{:S(2)}) collective-permute-start(bf16[4,64,768]{2,1,0:T(8,128)(2,1)} %get-tuple-element.84), channel_id=1, source_target_pairs={{0,64},{1,193},{2,66},{3,195},{4,68},{5,197},{6,70},{7,199},{8,72}... | collective-permute-start | bytes 1179656 | tf_op jit(solution)/shard_map/ppermute | solution.py:45
  184.1 0.9 copy-done.4
  185.0 2.3 add_halves.16
  187.2 0.9 copy-done.5
  188.1 2.2 add_halves.13
  190.4 0.7 copy-done.9
  191.1 1.9 add_halves.22
  193.0 1.5 collective-permute-start.27
  194.5 0.7 copy-done.10
  195.2 1.9 add_halves.19
  197.2 1.5 collective-permute-start.23
  198.7 0.7 copy-done.11
  199.4 2.0 add_halves.17
  201.5 0.7 copy-done.12
  202.2 2.0 add_halves.14
  204.2 1.3 collective-permute-start.16
  206.2 1.7 add_halves.23
  207.9 1.4 collective-permute-start.28
  210.0 1.7 add_halves.20
  211.7 2.7 %collective-permute-start.24 = (bf16[1,64,768]{2,1,0:T(8,128)(2,1)}, bf16[1,64,768]{2,1,0:T(8,128)(2,1)S(1)}, u32[]{:S(2)}, u32[]{:S(2)}) collective-permute-start(bf16[1,64,768]{2,1,0:T(8,128)(2,1)} %get-tuple-element.88), channel_id=1, source_target_pairs={{0,16},{1,49},{2,18},{3,51},{4,20},{5,53},{6,22},{7,55},{8,24},{9,... | collective-permute-start | bytes 294920 | tf_op jit(solution)/shard_map/ppermute | solution.py:45
  214.4 2.2 collective-permute-done.24.first_b
  217.3 1.9 last_down.1
  220.0 2.1 last_gate_up.1
  222.1 1.8 fusion.7
  (90 shorter events, 7.3 us)
Async XLA Ops:
  7.2 56.9 %all-gather.2.cloned.1.call-start = ((), (), s32[]{:S(2)}) async-start(), calls=%async_computation.1 | async-start | bytes 6893568 | tf_op jit(solution)/shard_map/all_gather | solution.py:296
  10.6 211.5 %reduce-scatter.2.cloned.1.call-start = ((), (), s32[]{:S(2)}) async-start(), calls=%async_computation.2 | async-start | bytes 3538944 | tf_op jit(solution)/shard_map/reduce_scatter | solution.py:425
  12.7 17.9 %copy-start.7 = (bf16[192,768]{1,0:T(8,128)(2,1)S(1)}, bf16[192,768]{1,0:T(8,128)(2,1)}, u32[]{:S(2)}) copy-start(bf16[192,768]{1,0:T(8,128)(2,1)} %get-tuple-element.52) | copy-start | bytes 884740
  12.7 7.7 %collective-permute-start = (bf16[1,192,768]{2,1,0:T(8,128)(2,1)}, bf16[1,192,768]{2,1,0:T(8,128)(2,1)S(1)}, u32[]{:S(2)}, u32[]{:S(2)}) collective-permute-start(bf16[1,192,768]{2,1,0:T(8,128)(2,1)} %bitcast.9), channel_id=1, source_target_pairs={{0,16},{1,49},{2,18},{3,51},{4,20},{5,53},{6,22},{7,55},{8,24},{9,... | collective-permute-start | bytes 884744 | tf_op jit(solution)/shard_map/ppermute | solution.py:45
  16.0 7.1 %collective-permute-start.4 = (bf16[1,192,768]{2,1,0:T(8,128)(2,1)}, bf16[1,192,768]{2,1,0:T(8,128)(2,1)S(1)}, u32[]{:S(2)}, u32[]{:S(2)}) collective-permute-start(bf16[1,192,768]{2,1,0:T(8,128)(2,1)} %bitcast.13), channel_id=1, source_target_pairs={{0,64},{1,193},{2,66},{3,195},{4,68},{5,197},{6,70},{7,199},{8,72}... | collective-permute-start | bytes 884744 | tf_op jit(solution)/shard_map/ppermute | solution.py:45
  21.4 9.2 %collective-permute-start.1 = (bf16[2,192,768]{2,1,0:T(8,128)(2,1)S(1)}, bf16[2,192,768]{2,1,0:T(8,128)(2,1)S(1)}, u32[]{:S(2)}, u32[]{:S(2)}) collective-permute-start(bf16[2,192,768]{2,1,0:T(8,128)(2,1)S(1)} %pad_maximum_fusion.6), channel_id=1, source_target_pairs={{0,48},{1,17},{2,50},{3,19},{4,52},{5,21},{6,54},{7,23},{8,56},{9,... | collective-permute-start | bytes 1769480 | tf_op jit(solution)/shard_map/ppermute | solution.py:45
  24.1 9.7 %copy-start.8 = (bf16[192,768]{1,0:T(8,128)(2,1)S(1)}, bf16[192,768]{1,0:T(8,128)(2,1)}, u32[]{:S(2)}) copy-start(bf16[192,768]{1,0:T(8,128)(2,1)} %get-tuple-element.53) | copy-start | bytes 884740
  24.1 9.7 %collective-permute-start.5 = (bf16[2,192,768]{2,1,0:T(8,128)(2,1)S(1)}, bf16[2,192,768]{2,1,0:T(8,128)(2,1)S(1)}, u32[]{:S(2)}, u32[]{:S(2)}) collective-permute-start(bf16[2,192,768]{2,1,0:T(8,128)(2,1)S(1)} %pad_maximum_fusion.7), channel_id=1, source_target_pairs={{0,192},{1,65},{2,194},{3,67},{4,196},{5,69},{6,198},{7,71},{8,200... | collective-permute-start | bytes 1769480 | tf_op jit(solution)/shard_map/ppermute | solution.py:45
  30.8 14.5 %collective-permute-start.2 = (bf16[4,128,768]{2,1,0:T(8,128)(2,1)S(1)}, bf16[4,128,768]{2,1,0:T(8,128)(2,1)S(1)}, u32[]{:S(2)}, u32[]{:S(2)}) collective-permute-start(bf16[4,128,768]{2,1,0:T(8,128)(2,1)S(1)} %slice.24), channel_id=1, source_target_pairs={{0,64},{1,193},{2,66},{3,195},{4,68},{5,197},{6,70},{7,199},{8,72}... | collective-permute-start | bytes 2359304 | tf_op jit(solution)/shard_map/ppermute | solution.py:45
  34.0 12.8 %collective-permute-start.6 = (bf16[4,128,768]{2,1,0:T(8,128)(2,1)S(1)}, bf16[4,128,768]{2,1,0:T(8,128)(2,1)S(1)}, u32[]{:S(2)}, u32[]{:S(2)}) collective-permute-start(bf16[4,128,768]{2,1,0:T(8,128)(2,1)S(1)} %slice.25), channel_id=1, source_target_pairs={{0,16},{1,49},{2,18},{3,51},{4,20},{5,53},{6,22},{7,55},{8,24},{9,... | collective-permute-start | bytes 2359304 | tf_op jit(solution)/shard_map/ppermute | solution.py:45
  46.7 26.6 %collective-permute-start.3 = (bf16[8,128,768]{2,1,0:T(8,128)(2,1)}, bf16[8,128,768]{2,1,0:T(8,128)(2,1)}, u32[]{:S(2)}, u32[]{:S(2)}) collective-permute-start(bf16[8,128,768]{2,1,0:T(8,128)(2,1)} %pad_maximum_fusion.g0), channel_id=1, source_target_pairs={{0,192},{1,65},{2,194},{3,67},{4,196},{5,69},{6,198},{7,71},{8,200... | collective-permute-start | bytes 4718600 | tf_op jit(solution)/shard_map/ppermute | solution.py:45
  48.2 25.2 %collective-permute-start.7 = (bf16[8,128,768]{2,1,0:T(8,128)(2,1)}, bf16[8,128,768]{2,1,0:T(8,128)(2,1)}, u32[]{:S(2)}, u32[]{:S(2)}) collective-permute-start(bf16[8,128,768]{2,1,0:T(8,128)(2,1)} %pad_maximum_fusion.1.u0), channel_id=1, source_target_pairs={{0,48},{1,17},{2,50},{3,19},{4,52},{5,21},{6,54},{7,23},{8,56},{9,... | collective-permute-start | bytes 4718600 | tf_op jit(solution)/shard_map/ppermute | solution.py:45
  48.2 3.7 %copy-start.20 = (s32[4]{0:T(128)S(1)}, s32[4]{0:T(128)}, u32[]{:S(2)}) copy-start(s32[4]{0:T(128)} %constant.51.clone) | copy-start | bytes 52
  48.2 3.7 %copy-start.21 = (s32[4]{0:T(128)S(1)}, s32[4]{0:T(128)}, u32[]{:S(2)}) copy-start(s32[4]{0:T(128)} %constant.52.clone) | copy-start | bytes 52
  48.2 8.3 %collective-permute-start.10 = (bf16[4,64,768]{2,1,0:T(8,128)(2,1)S(1)}, bf16[4,64,768]{2,1,0:T(8,128)(2,1)S(1)}, u32[]{:S(2)}, u32[]{:S(2)}) collective-permute-start(bf16[4,64,768]{2,1,0:T(8,128)(2,1)S(1)} %pad_maximum_fusion.8), channel_id=1, source_target_pairs={{0,16},{1,49},{2,18},{3,51},{4,20},{5,53},{6,22},{7,55},{8,24},{9,... | collective-permute-start | bytes 1179656 | tf_op jit(solution)/shard_map/ppermute | solution.py:45
  50.5 12.6 %collective-permute-start.8 = (bf16[4,64,768]{2,1,0:T(8,128)(2,1)S(1)}, bf16[4,64,768]{2,1,0:T(8,128)(2,1)S(1)}, u32[]{:S(2)}, u32[]{:S(2)}) collective-permute-start(bf16[4,64,768]{2,1,0:T(8,128)(2,1)S(1)} %pad_maximum_fusion.9), channel_id=1, source_target_pairs={{0,64},{1,193},{2,66},{3,195},{4,68},{5,197},{6,70},{7,199},{8,72}... | collective-permute-start | bytes 1179656 | tf_op jit(solution)/shard_map/ppermute | solution.py:45
  56.6 16.7 %copy-start.2 = (bf16[8,64,768]{2,1,0:T(8,128)(2,1)}, bf16[8,64,768]{2,1,0:T(8,128)(2,1)S(1)}, u32[]{:S(2)}) copy-start(bf16[8,64,768]{2,1,0:T(8,128)(2,1)S(1)} %pad_maximum_fusion.5.db0) | copy-start | bytes 2359300
  56.6 30.7 %collective-permute-start.11 = (bf16[8,64,768]{2,1,0:T(8,128)(2,1)S(1)}, bf16[8,64,768]{2,1,0:T(8,128)(2,1)S(1)}, u32[]{:S(2)}, u32[]{:S(2)}) collective-permute-start(bf16[8,64,768]{2,1,0:T(8,128)(2,1)S(1)} %pad_maximum_fusion.5.db0), channel_id=1, source_target_pairs={{0,48},{1,17},{2,50},{3,19},{4,52},{5,21},{6,54},{7,23},{8,56},{9,... | collective-permute-start | bytes 2359304 | tf_op jit(solution)/shard_map/ppermute | solution.py:45
  63.2 10.2 %copy-start.3 = (bf16[8,64,768]{2,1,0:T(8,128)(2,1)}, bf16[8,64,768]{2,1,0:T(8,128)(2,1)S(1)}, u32[]{:S(2)}) copy-start(bf16[8,64,768]{2,1,0:T(8,128)(2,1)S(1)} %pad_maximum_fusion.4.da0) | copy-start | bytes 2359300
  63.2 24.1 %collective-permute-start.9 = (bf16[8,64,768]{2,1,0:T(8,128)(2,1)S(1)}, bf16[8,64,768]{2,1,0:T(8,128)(2,1)}, u32[]{:S(2)}, u32[]{:S(2)}) collective-permute-start(bf16[8,64,768]{2,1,0:T(8,128)(2,1)S(1)} %pad_maximum_fusion.4.da0), channel_id=1, source_target_pairs={{0,192},{1,65},{2,194},{3,67},{4,196},{5,69},{6,198},{7,71},{8,200... | collective-permute-start | bytes 2359304 | tf_op jit(solution)/shard_map/ppermute | solution.py:45
  87.3 0.9 copy-start.13
  112.2 13.8 %collective-permute-start.12 = (bf16[384,4096]{1,0:T(8,128)(2,1)}, bf16[384,4096]{1,0:T(8,128)(2,1)S(1)}, u32[]{:S(2)}, u32[]{:S(2)}) collective-permute-start(bf16[384,4096]{1,0:T(8,128)(2,1)} %get-tuple-element.61), channel_id=1, source_target_pairs={{0,1},{1,0},{2,3},{3,2},{4,5},{5,4},{6,7},{7,6},{8,9},{9,8},{10,11... | collective-permute-start | bytes 9437192 | tf_op jit(solution)/shard_map/ppermute | solution.py:50
  140.3 19.9 %collective-permute-start.17 = (bf16[8,128,768]{2,1,0:T(8,128)(2,1)}, bf16[8,128,768]{2,1,0:T(8,128)(2,1)S(1)}, u32[]{:S(2)}, u32[]{:S(2)}) collective-permute-start(bf16[8,128,768]{2,1,0:T(8,128)(2,1)} %get-tuple-element.72), channel_id=1, source_target_pairs={{0,48},{1,17},{2,50},{3,19},{4,52},{5,21},{6,54},{7,23},{8,56},{9,... | collective-permute-start | bytes 4718600 | tf_op jit(solution)/shard_map/ppermute | solution.py:45
  140.4 25.1 %collective-permute-start.13 = (bf16[8,128,768]{2,1,0:T(8,128)(2,1)}, bf16[8,128,768]{2,1,0:T(8,128)(2,1)S(1)}, u32[]{:S(2)}, u32[]{:S(2)}) collective-permute-start(bf16[8,128,768]{2,1,0:T(8,128)(2,1)} %get-tuple-element.64), channel_id=1, source_target_pairs={{0,192},{1,65},{2,194},{3,67},{4,196},{5,69},{6,198},{7,71},{8,200... | collective-permute-start | bytes 4718600 | tf_op jit(solution)/shard_map/ppermute | solution.py:45
  140.5 31.5 %collective-permute-start.25 = (bf16[8,64,768]{2,1,0:T(8,128)(2,1)}, bf16[8,64,768]{2,1,0:T(8,128)(2,1)}, u32[]{:S(2)}, u32[]{:S(2)}) collective-permute-start(bf16[8,64,768]{2,1,0:T(8,128)(2,1)} %get-tuple-element.90), channel_id=1, source_target_pairs={{0,48},{1,17},{2,50},{3,19},{4,52},{5,21},{6,54},{7,23},{8,56},{9,... | collective-permute-start | bytes 2359304 | tf_op jit(solution)/shard_map/ppermute | solution.py:45
  141.8 35.2 %collective-permute-start.21 = (bf16[8,64,768]{2,1,0:T(8,128)(2,1)}, bf16[8,64,768]{2,1,0:T(8,128)(2,1)S(1)}, u32[]{:S(2)}, u32[]{:S(2)}) collective-permute-start(bf16[8,64,768]{2,1,0:T(8,128)(2,1)} %get-tuple-element.82), channel_id=1, source_target_pairs={{0,192},{1,65},{2,194},{3,67},{4,196},{5,69},{6,198},{7,71},{8,200... | collective-permute-start | bytes 2359304 | tf_op jit(solution)/shard_map/ppermute | solution.py:45
  160.2 1.3 copy-start.1
  165.5 18.6 %collective-permute-start.18 = (bf16[4,128,768]{2,1,0:T(8,128)(2,1)}, bf16[4,128,768]{2,1,0:T(8,128)(2,1)S(1)}, u32[]{:S(2)}, u32[]{:S(2)}) collective-permute-start(bf16[4,128,768]{2,1,0:T(8,128)(2,1)} %get-tuple-element.74), channel_id=1, source_target_pairs={{0,16},{1,49},{2,18},{3,51},{4,20},{5,53},{6,22},{7,55},{8,24},{9,... | collective-permute-start | bytes 2359304 | tf_op jit(solution)/shard_map/ppermute | solution.py:45
  165.5 1.2 copy-start
  170.7 16.5 %collective-permute-start.14 = (bf16[4,128,768]{2,1,0:T(8,128)(2,1)}, bf16[4,128,768]{2,1,0:T(8,128)(2,1)S(1)}, u32[]{:S(2)}, u32[]{:S(2)}) collective-permute-start(bf16[4,128,768]{2,1,0:T(8,128)(2,1)} %get-tuple-element.66), channel_id=1, source_target_pairs={{0,64},{1,193},{2,66},{3,195},{4,68},{5,197},{6,70},{7,199},{8,72}... | collective-permute-start | bytes 2359304 | tf_op jit(solution)/shard_map/ppermute | solution.py:45
  175.6 14.8 %collective-permute-start.26 = (bf16[4,64,768]{2,1,0:T(8,128)(2,1)}, bf16[4,64,768]{2,1,0:T(8,128)(2,1)S(1)}, u32[]{:S(2)}, u32[]{:S(2)}) collective-permute-start(bf16[4,64,768]{2,1,0:T(8,128)(2,1)} %get-tuple-element.92), channel_id=1, source_target_pairs={{0,16},{1,49},{2,18},{3,51},{4,20},{5,53},{6,22},{7,55},{8,24},{9,... | collective-permute-start | bytes 1179656 | tf_op jit(solution)/shard_map/ppermute | solution.py:45
  177.0 0.9 copy-start.6
  181.4 13.1 %collective-permute-start.22 = (bf16[4,64,768]{2,1,0:T(8,128)(2,1)}, bf16[4,64,768]{2,1,0:T(8,128)(2,1)S(1)}, u32[]{:S(2)}, u32[]{:S(2)}) collective-permute-start(bf16[4,64,768]{2,1,0:T(8,128)(2,1)} %get-tuple-element.84), channel_id=1, source_target_pairs={{0,64},{1,193},{2,66},{3,195},{4,68},{5,197},{6,70},{7,199},{8,72}... | collective-permute-start | bytes 1179656 | tf_op jit(solution)/shard_map/ppermute | solution.py:45
  184.1 0.9 copy-start.4
  187.2 11.5 %collective-permute-start.19 = (bf16[2,128,768]{2,1,0:T(8,128)(2,1)}, bf16[2,128,768]{2,1,0:T(8,128)(2,1)S(1)}, u32[]{:S(2)}, u32[]{:S(2)}) collective-permute-start(bf16[2,128,768]{2,1,0:T(8,128)(2,1)} %get-tuple-element.76), channel_id=1, source_target_pairs={{0,192},{1,65},{2,194},{3,67},{4,196},{5,69},{6,198},{7,71},{8,200... | collective-permute-start | bytes 1179656 | tf_op jit(solution)/shard_map/ppermute | solution.py:45
  187.2 0.9 copy-start.5
  190.3 11.1 %collective-permute-start.15 = (bf16[2,128,768]{2,1,0:T(8,128)(2,1)}, bf16[2,128,768]{2,1,0:T(8,128)(2,1)S(1)}, u32[]{:S(2)}, u32[]{:S(2)}) collective-permute-start(bf16[2,128,768]{2,1,0:T(8,128)(2,1)} %get-tuple-element.68), channel_id=1, source_target_pairs={{0,48},{1,17},{2,50},{3,19},{4,52},{5,21},{6,54},{7,23},{8,56},{9,... | collective-permute-start | bytes 1179656 | tf_op jit(solution)/shard_map/ppermute | solution.py:45
  190.4 0.8 copy-start.9
  193.0 12.5 %collective-permute-start.27 = (bf16[2,64,768]{2,1,0:T(8,128)(2,1)}, bf16[2,64,768]{2,1,0:T(8,128)(2,1)S(1)}, u32[]{:S(2)}, u32[]{:S(2)}) collective-permute-start(bf16[2,64,768]{2,1,0:T(8,128)(2,1)} %get-tuple-element.94), channel_id=1, source_target_pairs={{0,192},{1,65},{2,194},{3,67},{4,196},{5,69},{6,198},{7,71},{8,200... | collective-permute-start | bytes 589832 | tf_op jit(solution)/shard_map/ppermute | solution.py:45
  194.5 0.8 copy-start.10
  197.2 12.1 %collective-permute-start.23 = (bf16[2,64,768]{2,1,0:T(8,128)(2,1)}, bf16[2,64,768]{2,1,0:T(8,128)(2,1)S(1)}, u32[]{:S(2)}, u32[]{:S(2)}) collective-permute-start(bf16[2,64,768]{2,1,0:T(8,128)(2,1)} %get-tuple-element.86), channel_id=1, source_target_pairs={{0,48},{1,17},{2,50},{3,19},{4,52},{5,21},{6,54},{7,23},{8,56},{9,... | collective-permute-start | bytes 589832 | tf_op jit(solution)/shard_map/ppermute | solution.py:45
  198.7 0.8 copy-start.11
  201.4 17.8 %collective-permute-start.20 = (bf16[1,128,768]{2,1,0:T(8,128)(2,1)}, bf16[1,128,768]{2,1,0:T(8,128)(2,1)S(1)}, u32[]{:S(2)}, u32[]{:S(2)}) collective-permute-start(bf16[1,128,768]{2,1,0:T(8,128)(2,1)} %get-tuple-element.78), channel_id=1, source_target_pairs={{0,64},{1,193},{2,66},{3,195},{4,68},{5,197},{6,70},{7,199},{8,72}... | collective-permute-start | bytes 589832 | tf_op jit(solution)/shard_map/ppermute | solution.py:45
  201.5 0.7 copy-start.12
  204.2 15.0 %collective-permute-start.16 = (bf16[1,128,768]{2,1,0:T(8,128)(2,1)}, bf16[1,128,768]{2,1,0:T(8,128)(2,1)S(1)}, u32[]{:S(2)}, u32[]{:S(2)}) collective-permute-start(bf16[1,128,768]{2,1,0:T(8,128)(2,1)} %get-tuple-element.70), channel_id=1, source_target_pairs={{0,16},{1,49},{2,18},{3,51},{4,20},{5,53},{6,22},{7,55},{8,24},{9,... | collective-permute-start | bytes 589832 | tf_op jit(solution)/shard_map/ppermute | solution.py:45
  205.5 0.7 copy-start.14
  207.9 6.5 %collective-permute-start.28 = (bf16[1,64,768]{2,1,0:T(8,128)(2,1)}, bf16[1,64,768]{2,1,0:T(8,128)(2,1)S(1)}, u32[]{:S(2)}, u32[]{:S(2)}) collective-permute-start(bf16[1,64,768]{2,1,0:T(8,128)(2,1)} %get-tuple-element.96), channel_id=1, source_target_pairs={{0,64},{1,193},{2,66},{3,195},{4,68},{5,197},{6,70},{7,199},{8,72}... | collective-permute-start | bytes 294920 | tf_op jit(solution)/shard_map/ppermute | solution.py:45
  209.3 0.7 copy-start.15
  211.7 4.9 %collective-permute-start.24 = (bf16[1,64,768]{2,1,0:T(8,128)(2,1)}, bf16[1,64,768]{2,1,0:T(8,128)(2,1)S(1)}, u32[]{:S(2)}, u32[]{:S(2)}) collective-permute-start(bf16[1,64,768]{2,1,0:T(8,128)(2,1)} %get-tuple-element.88), channel_id=1, source_target_pairs={{0,16},{1,49},{2,18},{3,51},{4,20},{5,53},{6,22},{7,55},{8,24},{9,... | collective-permute-start | bytes 294920 | tf_op jit(solution)/shard_map/ppermute | solution.py:45
  214.4 2.2 copy-start.18
  216.6 0.6 copy-start.19
  219.2 0.7 copy-start.16
  219.2 0.7 copy-start.17
Sparse Core Ops, SparseCore 0:
  10.8 51.1 all-gather.1
  130.9 42.5 reduce-scatter.1
